TPU v7x, 32 devices: a whole 2x2x4 slice. The times are simulated.
32 devices in a mesh: wide: 8 (over z, x), lend: 4 (over y, core).
Axes of the slice: x: 2, y: 2, z: 4, core: 2. Of those that a mesh axis runs over, the one named last changes fastest.
Arguments:
- operators: bfloat16 [4, 8, 1024, 1024], P('lend', 'wide'), as said below
- dual_rhs: float32 [4, 4096, 128], P('lend', 'wide'), may hold values from -6 to 6
- contact: int32 [4, 4096], P('lend', 'wide'), may hold values 0 or 1
- costs: int32 [4, 8], P('lend', 'wide'), may hold values from 1 to 8, as said below
Outputs:
- multipliers: float32 [4, 4096, 128], P('lend', 'wide')
- gradient: float32 [4, 4096, 128], P('lend', 'wide')
Inputs may be any that keep to these rules, and one draw needn't show every extreme that they name: `operators`: each subdomain's operator is symmetric positive definite up to rounding. 1 marks a contact multiplier that must stay nonnegative, 0 a gluing one. The number of live blocks of 128 slots of each subdomain; its live slots are the first costs * 128. For every j, costs[2 j, w] + costs[2 j + 1, w] is at most 9.
All inputs are finite; a program needn't handle non-finite values. No bound on the sum of `contact` on one device may be relied on, other than what follows from the above.
Results may differ from a plain program's by a relative error of at most 0.0086.
Values may be sent and summed in bfloat16 or wider, within the bound.
A program may use at most 64 MiB of HBM per device.

v0:
```python
import jax
import jax.numpy as jnp
from jax import lax
from jax.sharding import PartitionSpec as P

ROWBLK = 128
ITERS = 4


RIDGE = 1.0
FIRST_STEP = 0.1
EPSILON = 1e-06


def from_behind(block, axis, distance):
    devices = range(lax.axis_size(axis))
    route = [((i - distance) % len(devices), i) for i in devices]
    return lax.ppermute(block, axis, route)


def project(values, bounded):
    return jnp.where(bounded, jnp.maximum(values, 0.0), values)


def block_product(matrix, vectors, start_block, stop_block):
    order = matrix.shape[0]

    def add_block(number, result):
        offset = number * ROWBLK
        rows_here = lax.dynamic_slice_in_dim(matrix, offset, ROWBLK, 0)
        piece = jnp.dot(rows_here, vectors, preferred_element_type=jnp.float32)
        return lax.dynamic_update_slice_in_dim(result, piece, offset, 0)

    empty = jnp.zeros((order, vectors.shape[1]), jnp.float32)
    return lax.fori_loop(start_block, stop_block, add_block, empty)


def on_device(operators, dual_rhs, contact, costs):
    matrix = operators[0, 0]
    rhs_own = dual_rhs[0]
    bounded = (contact[0] == 1)[:, None]
    live = costs[0, 0]
    order = matrix.shape[0]
    face = order // 2
    slots = lax.broadcasted_iota(jnp.int32, (order, 1), 0)
    active = slots < live * ROWBLK
    multipliers = jnp.zeros_like(rhs_own)
    image = jnp.zeros_like(rhs_own)
    gradient = -rhs_own
    steplen = jnp.full((1, rhs_own.shape[1]), FIRST_STEP, jnp.float32)
    for iteration in range(ITERS):
        finished = iteration + 1 == ITERS
        moved = project(multipliers - steplen * gradient, bounded)
        change = moved - multipliers
        squares = jnp.sum(change * change, axis=0)
        if not finished:
            numer = lax.psum(squares, "wide")
        step_half = change.astype(jnp.bfloat16)
        previous = from_behind(step_half, "wide", 1)
        dual_operand = jnp.concatenate([-previous, step_half], axis=0)
        dual_operand = jnp.where(active, dual_operand, jnp.zeros_like(dual_operand))
        product = block_product(matrix, dual_operand, 0, live)
        returned = from_behind(product[:face], "wide", -1)
        response = product[face:] - returned + RIDGE * change
        image = image + response
        gradient = image - rhs_own
        multipliers = moved
        if not finished:
            bending = jnp.sum(change * response, axis=0)
            denom = lax.psum(bending, "wide")
            steplen = ((numer + EPSILON) / (denom + EPSILON))[None, :]
    return (multipliers[None], gradient[None])


def solution(mesh):
    return jax.shard_map(
        on_device,
        mesh=mesh,
        in_specs=(
            P("lend", "wide", None, None),
            P("lend", "wide", None),
            P("lend", "wide"),
            P("lend", "wide"),
        ),
        out_specs=(P("lend", "wide", None), P("lend", "wide", None)),
        check_vma=False,
    )
```

profile of v0, /device:TPU:0, one launch (start us, length us, event | category | flops | bytes accessed | tf_op | source)
XLA Modules:
  0.0 187.3 jit_solution(8703514754990308063)
XLA Ops:
  2.4 3.0 %collective-permute-start = (bf16[512,128]{1,0:T(8,128)(2,1)S(1)}, bf16[512,128]{1,0:T(8,128)(2,1)S(1)}, u32[]{:S(2)}, u32[]{:S(2)}) collective-permute-start(bf16[512,128]{1,0:T(8,128)(2,1)S(1)} %fusion.23), channel_id=1, source_target_pairs={{28,0},{0,4},{4,8},{8,12},{12,16},{16,20},{20,24},{24,28},{29,1},{... | collective-permute-start | bytes 393224 | tf_op jit(solution)/shard_map/ppermute | solution.py:18
  6.1 5.9 %collective-permute-done = bf16[512,128]{1,0:T(8,128)(2,1)S(1)} collective-permute-done((bf16[512,128]{1,0:T(8,128)(2,1)S(1)}, bf16[512,128]{1,0:T(8,128)(2,1)S(1)}, u32[]{:S(2)}, u32[]{:S(2)}) %collective-permute-start) | collective-permute-done | bytes 131104 | tf_op jit(solution)/shard_map/ppermute | solution.py:18
  12.2 15.4 %while.40 = (s32[]{:T(128)}, f32[1024,128]{1,0:T(8,128)S(1)}, s32[]{:T(128)}, bf16[1024,1024]{1,0:T(8,128)(2,1)}, bf16[1024,128]{1,0:T(8,128)(2,1)S(1)}, /*index=5*/s32[]{:T(128)}, s32[]{:T(128)}, s32[]{:T(128)}, s32[]{:T(128)}) while((s32[]{:T(128)}, f32[1024,128]{1,0:T(8,128)S(1)}, s32[]{:T(128)}, bf16[1024,1024]{1,0:T(8,128)(2,1)}, ...), condition=%wide.region_3.4_spmd, body=%wide.region_2.3_spmd.sunk | while | flops 33554436 | bytes 590987 | solution.py:35
  12.9 1.2 convolution_dynamic-update-slice_fusion.8
  14.8 1.2 convolution_dynamic-update-slice_fusion.8
  16.6 1.2 convolution_dynamic-update-slice_fusion.8
  18.5 1.2 convolution_dynamic-update-slice_fusion.8
  20.3 1.2 convolution_dynamic-update-slice_fusion.8
  22.2 1.2 convolution_dynamic-update-slice_fusion.8
  24.0 1.2 convolution_dynamic-update-slice_fusion.8
  25.9 1.2 convolution_dynamic-update-slice_fusion.8
  27.8 6.4 %collective-permute-done.1 = f32[512,128]{1,0:T(8,128)S(1)} collective-permute-done((f32[512,128]{1,0:T(8,128)S(1)}, f32[512,128]{1,0:T(8,128)S(1)}, u32[]{:S(2)}, u32[]{:S(2)}) %collective-permute-start.1) | collective-permute-done | bytes 262176 | tf_op jit(solution)/shard_map/ppermute | solution.py:18
  34.4 19.9 %all-reduce.2 = (f32[128]{0:T(128)S(1)}, f32[128]{0:T(128)S(1)}) all-reduce(f32[128]{0:T(128)S(1)} %get-tuple-element.119, f32[128]{0:T(128)S(1)} %get-tuple-element.118), channel_id=1, replica_groups=mesh['wide'=8,'lend'=4] {'wide'}, use_global_device_ids=true, to_apply=%region_5.6 | all-reduce | flops 256 | bytes 2048 | tf_op jit(solution)/shard_map/psum | solution.py:70
  54.5 7.8 %collective-permute-done.2 = bf16[512,128]{1,0:T(8,128)(2,1)S(1)} collective-permute-done((bf16[512,128]{1,0:T(8,128)(2,1)S(1)}, bf16[512,128]{1,0:T(8,128)(2,1)S(1)}, u32[]{:S(2)}, u32[]{:S(2)}) %collective-permute-start.2) | collective-permute-done | bytes 131104 | tf_op jit(solution)/shard_map/ppermute | solution.py:18
  62.5 15.4 %while.41 = (s32[]{:T(128)}, f32[1024,128]{1,0:T(8,128)S(1)}, s32[]{:T(128)}, bf16[1024,1024]{1,0:T(8,128)(2,1)}, bf16[1024,128]{1,0:T(8,128)(2,1)S(1)}, /*index=5*/s32[]{:T(128)}, s32[]{:T(128)}, s32[]{:T(128)}, s32[]{:T(128)}) while((s32[]{:T(128)}, f32[1024,128]{1,0:T(8,128)S(1)}, s32[]{:T(128)}, bf16[1024,1024]{1,0:T(8,128)(2,1)}, ...), condition=%wide.region_9.10_spmd, body=%wide.region_8.9_spmd.sunk | while | flops 33554436 | bytes 590987 | solution.py:35
  63.2 1.2 convolution_dynamic-update-slice_fusion.9
  65.0 1.2 convolution_dynamic-update-slice_fusion.9
  66.9 1.2 convolution_dynamic-update-slice_fusion.9
  68.7 1.2 convolution_dynamic-update-slice_fusion.9
  70.6 1.2 convolution_dynamic-update-slice_fusion.9
  72.4 1.2 convolution_dynamic-update-slice_fusion.9
  74.3 1.2 convolution_dynamic-update-slice_fusion.9
  76.1 1.2 convolution_dynamic-update-slice_fusion.9
  78.0 7.8 %collective-permute-done.3 = f32[512,128]{1,0:T(8,128)S(1)} collective-permute-done((f32[512,128]{1,0:T(8,128)S(1)}, f32[512,128]{1,0:T(8,128)S(1)}, u32[]{:S(2)}, u32[]{:S(2)}) %collective-permute-start.3) | collective-permute-done | bytes 262176 | tf_op jit(solution)/shard_map/ppermute | solution.py:18
  85.9 18.5 %all-reduce.1 = (f32[128]{0:T(128)S(1)}, f32[128]{0:T(128)S(1)}) all-reduce(f32[128]{0:T(128)S(1)} %get-tuple-element.123, f32[128]{0:T(128)S(1)} %get-tuple-element.122), channel_id=1, replica_groups=mesh['wide'=8,'lend'=4] {'wide'}, use_global_device_ids=true, to_apply=%region_11.12 | all-reduce | flops 256 | bytes 2048 | tf_op jit(solution)/shard_map/psum | solution.py:70
  105.3 7.0 %collective-permute-done.4 = bf16[512,128]{1,0:T(8,128)(2,1)S(1)} collective-permute-done((bf16[512,128]{1,0:T(8,128)(2,1)S(1)}, bf16[512,128]{1,0:T(8,128)(2,1)S(1)}, u32[]{:S(2)}, u32[]{:S(2)}) %collective-permute-start.4) | collective-permute-done | bytes 131104 | tf_op jit(solution)/shard_map/ppermute | solution.py:18
  112.7 15.4 %while.42 = (s32[]{:T(128)}, f32[1024,128]{1,0:T(8,128)S(1)}, s32[]{:T(128)}, bf16[1024,1024]{1,0:T(8,128)(2,1)}, bf16[1024,128]{1,0:T(8,128)(2,1)S(1)}, /*index=5*/s32[]{:T(128)}, s32[]{:T(128)}, s32[]{:T(128)}, s32[]{:T(128)}) while((s32[]{:T(128)}, f32[1024,128]{1,0:T(8,128)S(1)}, s32[]{:T(128)}, bf16[1024,1024]{1,0:T(8,128)(2,1)}, ...), condition=%wide.region_15.16_spmd, body=%wide.region_14.15_spmd.sunk | while | flops 33554436 | bytes 590987 | solution.py:35
  113.3 1.2 convolution_dynamic-update-slice_fusion.10
  115.2 1.2 convolution_dynamic-update-slice_fusion.10
  117.0 1.2 convolution_dynamic-update-slice_fusion.10
  118.8 1.2 convolution_dynamic-update-slice_fusion.10
  120.7 1.2 convolution_dynamic-update-slice_fusion.10
  122.5 1.2 convolution_dynamic-update-slice_fusion.10
  124.4 1.2 convolution_dynamic-update-slice_fusion.10
  126.2 1.2 convolution_dynamic-update-slice_fusion.10
  128.2 8.7 %collective-permute-done.5 = f32[512,128]{1,0:T(8,128)S(1)} collective-permute-done((f32[512,128]{1,0:T(8,128)S(1)}, f32[512,128]{1,0:T(8,128)S(1)}, u32[]{:S(2)}, u32[]{:S(2)}) %collective-permute-start.5) | collective-permute-done | bytes 262176 | tf_op jit(solution)/shard_map/ppermute | solution.py:18
  136.9 19.3 %all-reduce = (f32[128]{0:T(128)S(1)}, f32[128]{0:T(128)S(1)}) all-reduce(f32[128]{0:T(128)S(1)} %get-tuple-element.121, f32[128]{0:T(128)S(1)} %get-tuple-element.120), channel_id=1, replica_groups=mesh['wide'=8,'lend'=4] {'wide'}, use_global_device_ids=true, to_apply=%region_17.18 | all-reduce | flops 256 | bytes 2048 | tf_op jit(solution)/shard_map/psum | solution.py:70
  156.5 7.7 %collective-permute-done.6 = bf16[512,128]{1,0:T(8,128)(2,1)S(1)} collective-permute-done((bf16[512,128]{1,0:T(8,128)(2,1)S(1)}, bf16[512,128]{1,0:T(8,128)(2,1)S(1)}, u32[]{:S(2)}, u32[]{:S(2)}) %collective-permute-start.6) | collective-permute-done | bytes 131104 | tf_op jit(solution)/shard_map/ppermute | solution.py:18
  164.4 15.4 %while.43 = (s32[]{:T(128)}, f32[1024,128]{1,0:T(8,128)S(1)}, s32[]{:T(128)}, bf16[1024,1024]{1,0:T(8,128)(2,1)}, bf16[1024,128]{1,0:T(8,128)(2,1)S(1)}, /*index=5*/s32[]{:T(128)}, s32[]{:T(128)}, s32[]{:T(128)}, s32[]{:T(128)}) while((s32[]{:T(128)}, f32[1024,128]{1,0:T(8,128)S(1)}, s32[]{:T(128)}, bf16[1024,1024]{1,0:T(8,128)(2,1)}, ...), condition=%wide.region_19.20_spmd, body=%wide.region_18.19_spmd.sunk | while | flops 33554436 | bytes 590987 | solution.py:35
  165.1 1.2 convolution_dynamic-update-slice_fusion.11
  166.9 1.2 convolution_dynamic-update-slice_fusion.11
  168.8 1.2 convolution_dynamic-update-slice_fusion.11
  170.6 1.2 convolution_dynamic-update-slice_fusion.11
  172.5 1.2 convolution_dynamic-update-slice_fusion.11
  174.3 1.2 convolution_dynamic-update-slice_fusion.11
  176.2 1.2 convolution_dynamic-update-slice_fusion.11
  178.0 1.2 convolution_dynamic-update-slice_fusion.11
  179.9 6.4 %collective-permute-done.7 = f32[512,128]{1,0:T(8,128)S(1)} collective-permute-done((f32[512,128]{1,0:T(8,128)S(1)}, f32[512,128]{1,0:T(8,128)S(1)}, u32[]{:S(2)}, u32[]{:S(2)}) %collective-permute-start.7) | collective-permute-done | bytes 262176 | tf_op jit(solution)/shard_map/ppermute | solution.py:18
  (38 shorter events, 5.9 us)
Async XLA Ops:
  2.4 9.5 %collective-permute-start = (bf16[512,128]{1,0:T(8,128)(2,1)S(1)}, bf16[512,128]{1,0:T(8,128)(2,1)S(1)}, u32[]{:S(2)}, u32[]{:S(2)}) collective-permute-start(bf16[512,128]{1,0:T(8,128)(2,1)S(1)} %fusion.23), channel_id=1, source_target_pairs={{28,0},{0,4},{4,8},{8,12},{12,16},{16,20},{20,24},{24,28},{29,1},{... | collective-permute-start | bytes 393224 | tf_op jit(solution)/shard_map/ppermute | solution.py:18
  12.2 22.0 %copy-start = (f32[1,512,128]{2,1,0:T(8,128)S(1)}, f32[1,512,128]{2,1,0:T(8,128)}, u32[]{:S(2)}) copy-start(f32[1,512,128]{2,1,0:T(8,128)} %param.13) | copy-start | bytes 786436
  27.7 6.5 %collective-permute-start.1 = (f32[512,128]{1,0:T(8,128)S(1)}, f32[512,128]{1,0:T(8,128)S(1)}, u32[]{:S(2)}, u32[]{:S(2)}) collective-permute-start(f32[512,128]{1,0:T(8,128)S(1)} %slice.25), channel_id=1, source_target_pairs={{4,0},{8,4},{12,8},{16,12},{20,16},{24,20},{28,24},{0,28},{5,1},{9... | collective-permute-start | bytes 786440 | tf_op jit(solution)/shard_map/ppermute | solution.py:18
  54.4 7.8 %collective-permute-start.2 = (bf16[512,128]{1,0:T(8,128)(2,1)S(1)}, bf16[512,128]{1,0:T(8,128)(2,1)S(1)}, u32[]{:S(2)}, u32[]{:S(2)}) collective-permute-start(bf16[512,128]{1,0:T(8,128)(2,1)S(1)} %get-tuple-element.176), channel_id=1, source_target_pairs={{28,0},{0,4},{4,8},{8,12},{12,16},{16,20},{20,24},{24,28},{29,1},{... | collective-permute-start | bytes 393224 | tf_op jit(solution)/shard_map/ppermute | solution.py:18
  78.0 7.8 %collective-permute-start.3 = (f32[512,128]{1,0:T(8,128)S(1)}, f32[512,128]{1,0:T(8,128)S(1)}, u32[]{:S(2)}, u32[]{:S(2)}) collective-permute-start(f32[512,128]{1,0:T(8,128)S(1)} %slice.27), channel_id=1, source_target_pairs={{4,0},{8,4},{12,8},{16,12},{20,16},{24,20},{28,24},{0,28},{5,1},{9... | collective-permute-start | bytes 786440 | tf_op jit(solution)/shard_map/ppermute | solution.py:18
  104.6 7.8 %collective-permute-start.4 = (bf16[512,128]{1,0:T(8,128)(2,1)S(1)}, bf16[512,128]{1,0:T(8,128)(2,1)S(1)}, u32[]{:S(2)}, u32[]{:S(2)}) collective-permute-start(bf16[512,128]{1,0:T(8,128)(2,1)S(1)} %get-tuple-element.172), channel_id=1, source_target_pairs={{28,0},{0,4},{4,8},{8,12},{12,16},{16,20},{20,24},{24,28},{29,1},{... | collective-permute-start | bytes 393224 | tf_op jit(solution)/shard_map/ppermute | solution.py:18
  128.1 8.7 %collective-permute-start.5 = (f32[512,128]{1,0:T(8,128)S(1)}, f32[512,128]{1,0:T(8,128)S(1)}, u32[]{:S(2)}, u32[]{:S(2)}) collective-permute-start(f32[512,128]{1,0:T(8,128)S(1)} %slice.29), channel_id=1, source_target_pairs={{4,0},{8,4},{12,8},{16,12},{20,16},{24,20},{28,24},{0,28},{5,1},{9... | collective-permute-start | bytes 786440 | tf_op jit(solution)/shard_map/ppermute | solution.py:18
  156.4 7.7 %collective-permute-start.6 = (bf16[512,128]{1,0:T(8,128)(2,1)S(1)}, bf16[512,128]{1,0:T(8,128)(2,1)S(1)}, u32[]{:S(2)}, u32[]{:S(2)}) collective-permute-start(bf16[512,128]{1,0:T(8,128)(2,1)S(1)} %get-tuple-element.170), channel_id=1, source_target_pairs={{28,0},{0,4},{4,8},{8,12},{12,16},{16,20},{20,24},{24,28},{29,1},{... | collective-permute-start | bytes 393224 | tf_op jit(solution)/shard_map/ppermute | solution.py:18
  179.9 6.4 %collective-permute-start.7 = (f32[512,128]{1,0:T(8,128)S(1)}, f32[512,128]{1,0:T(8,128)S(1)}, u32[]{:S(2)}, u32[]{:S(2)}) collective-permute-start(f32[512,128]{1,0:T(8,128)S(1)} %slice.31), channel_id=1, source_target_pairs={{4,0},{8,4},{12,8},{16,12},{20,16},{24,20},{28,24},{0,28},{5,1},{9... | collective-permute-start | bytes 786440 | tf_op jit(solution)/shard_map/ppermute | solution.py:18
where the time goes:
time: 188 us; the launch traced here: 187 us
  blocking collectives  57.7 us (31%)
  waiting for transfers between devices  57.5 us (31%)
  matrix products  37.5 us (20%)
  loops' own time  24.2 us (13%)
  other arithmetic  4.6 us (2%)
  starting transfers between devices  4.06 us (2%)
    psum x3, blocking collectives, on_device(): denom = lax.psum(bending, 'wide')  57.7 us
    ppermute x8, waiting for transfers between devices, from_behind(): return lax.ppermute(block, axis, route)  57.5 us
    dot_general x32, matrix products, add_block(): piece = jnp.dot(rows_here, vectors, preferred_element_type=jnp.float32)  37.5 us
    another operation x4, loops' own time, block_product(): return lax.fori_loop(start_block, stop_block, add_block, empty)  24.2 us
    ppermute x8, starting transfers between devices, from_behind(): return lax.ppermute(block, axis, route)  4.06 us
  transfers between devices with their start and end apart: 8, of which 8 were waited for; matrix products, arithmetic and copies ran while one was open for 0% of the time, Pallas kernels for 0%

commit v1 on v0

v1 whole, which is shorter than its diff:
```python
import functools

import jax
import jax.numpy as jnp
from jax import lax
from jax.experimental import pallas as pl
from jax.experimental.pallas import tpu as pltpu
from jax.sharding import PartitionSpec as P

ROWBLK = 128
ITERS = 4
RIDGE = 1.0
FIRST_STEP = 0.1
EPSILON = 1e-06
PIECES = 2
MESH = pl.DeviceIdType.MESH


def kernel(
    n,
    op_hbm,
    rhs_hbm,
    contact_ref,
    costs_ref,
    lam_hbm,
    grad_hbm,
    op,
    rhs,
    rhs_send,
    rhs_recv,
    contact_recv,
    floor,
    lam,
    grad,
    operand,
    y_send,
    y_recv,
    part_send,
    part_recv,
    load_sem,
    out_sem,
    first_send_sem,
    first_recv_sem,
    y_send_sem,
    y_recv_sem,
    part_send_sem,
    part_recv_sem,
):
    order, cases = operand.shape
    face = order // 2
    piece = face // PIECES
    me = lax.axis_index("wide")
    right = lax.rem(me + 1, n)
    left = lax.rem(me + n - 1, n)

    load_rhs = pltpu.make_async_copy(rhs_hbm.at[0], rhs, load_sem.at[0])
    load_rhs.start()
    load_op = pltpu.make_async_copy(op_hbm.at[0, 0], op, load_sem.at[1])
    load_op.start()

    barrier = pltpu.get_barrier_semaphore()
    for d in range(1, n):
        pl.semaphore_signal(
            barrier, inc=1, device_id={"wide": lax.rem(me + d, n)}, device_id_type=MESH
        )

    live = costs_ref[0, 0] * ROWBLK

    def active(start, rows):
        return lax.broadcasted_iota(jnp.int32, (rows, cases), 0) + start < live

    def make_floor(flags, base):
        for start in range(0, face, ROWBLK):
            row = flags[:, start : start + ROWBLK]
            row = jnp.where(row == 1, 0.0, -jnp.inf).astype(jnp.float32)
            floor[base + start : base + start + ROWBLK, :] = jnp.broadcast_to(
                row, (cases, ROWBLK)
            ).T

    load_rhs.wait()
    for p in range(PIECES):
        rows = slice(p * piece, (p + 1) * piece)
        rhs_send[rows, :] = rhs[rows, :].astype(jnp.bfloat16)

    pl.semaphore_wait(barrier, n - 1)

    sent = []
    first = []
    copy = pltpu.make_async_remote_copy(
        src_ref=contact_ref,
        dst_ref=contact_recv,
        send_sem=first_send_sem.at[PIECES],
        recv_sem=first_recv_sem.at[PIECES],
        device_id={"wide": right},
        device_id_type=MESH,
    )
    copy.start()
    contact_copy = copy
    sent.append(copy)
    for p in range(PIECES):
        rows = pl.ds(p * piece, piece)
        copy = pltpu.make_async_remote_copy(
            src_ref=rhs_send.at[rows],
            dst_ref=rhs_recv.at[rows],
            send_sem=first_send_sem.at[p],
            recv_sem=first_recv_sem.at[p],
            device_id={"wide": right},
            device_id_type=MESH,
        )
        copy.start()
        first.append(copy)
        sent.append(copy)

    make_floor(contact_ref, face)
    steplen = jnp.full((1, cases), FIRST_STEP, jnp.float32)
    arrivals = None
    for it in range(ITERS):
        finished = it + 1 == ITERS
        squares = jnp.zeros((8, cases), jnp.float32)
        for own in (True, False):
            base = face if own else 0
            if it == 0 and not own:
                contact_copy.wait_recv()
                make_floor(contact_recv, 0)
            for start in range(0, face, ROWBLK):
                at = slice(base + start, base + start + ROWBLK)
                here = slice(start, start + ROWBLK)
                fresh = start % piece == 0
                if it == 0:
                    if own:
                        g = -rhs[here, :]
                    else:
                        if fresh:
                            first[start // piece].wait_recv()
                        g = -rhs_recv[here, :].astype(jnp.float32)
                    before = jnp.zeros_like(g)
                else:
                    other = 0 if own else face
                    if fresh:
                        arrivals[(other + start) // piece].wait_recv()
                    there = slice(other + start, other + start + ROWBLK)
                    came = y_recv[it - 1, there, :].astype(jnp.float32)
                    g = grad[at, :] - came if own else grad[at, :] + came
                    before = lam[at, :]
                moved = jnp.maximum(before - steplen * g, floor[at, :])
                change = moved - before
                lam[at, :] = moved
                grad[at, :] = g + RIDGE * change
                if own:
                    squares += jnp.sum(
                        (change * change).reshape(ROWBLK // 8, 8, cases), axis=0
                    )
                signed = change if own else -change
                operand[at, :] = jnp.where(
                    active(base + start, ROWBLK), signed, 0.0
                ).astype(jnp.bfloat16)
        if finished:
            save_lam = pltpu.make_async_copy(
                lam.at[pl.ds(face, face)], lam_hbm.at[0], out_sem.at[0]
            )
            save_lam.start()
        if it == 0:
            load_op.wait()
        bending = RIDGE * squares
        next_arrivals = {}
        for p in range(PIECES):
            for base in (0, face):
                start = base + p * piece
                at = slice(start, start + piece)
                vectors = operand[...]
                y = jnp.dot(op[at, :], vectors, preferred_element_type=jnp.float32)
                y = jnp.where(active(start, piece), y, 0.0)
                if not finished or base == 0:
                    y_send[it, at, :] = y.astype(jnp.bfloat16)
                    copy = pltpu.make_async_remote_copy(
                        src_ref=y_send.at[it, pl.ds(start, piece)],
                        dst_ref=y_recv.at[it, pl.ds(start, piece)],
                        send_sem=y_send_sem.at[it, start // piece],
                        recv_sem=y_recv_sem.at[it, start // piece],
                        device_id={"wide": left if base == 0 else right},
                        device_id_type=MESH,
                    )
                    copy.start()
                    sent.append(copy)
                    next_arrivals[start // piece] = copy
                if base == 0:
                    if not finished:
                        grad[at, :] = grad[at, :] - y
                else:
                    grad[at, :] = grad[at, :] + y
                if not finished:
                    bending += jnp.sum(
                        (operand[at, :].astype(jnp.float32) * y).reshape(
                            piece // 8, 8, cases
                        ),
                        axis=0,
                    )
        arrivals = next_arrivals
        if not finished:
            mine = jnp.concatenate(
                [
                    jnp.sum(squares, axis=0, keepdims=True),
                    jnp.sum(bending, axis=0, keepdims=True),
                ],
                axis=0,
            )
            part_send[it] = mine
            parts = []
            for d in range(1, n):
                copy = pltpu.make_async_remote_copy(
                    src_ref=part_send.at[it],
                    dst_ref=part_recv.at[it, d],
                    send_sem=part_send_sem.at[it, d],
                    recv_sem=part_recv_sem.at[it, d],
                    device_id={"wide": lax.rem(me + d, n)},
                    device_id_type=MESH,
                )
                copy.start()
                parts.append(copy)
                sent.append(copy)
            total = mine
            for d in range(1, n):
                parts[d - 1].wait_recv()
                total = total + part_recv[it, d]
            steplen = (total[0:1] + EPSILON) / (total[1:2] + EPSILON)

    saves = [save_lam]
    for p in range(PIECES):
        arrivals[p].wait_recv()
        at = slice(face + p * piece, face + (p + 1) * piece)
        here = slice(p * piece, (p + 1) * piece)
        grad[at, :] = grad[at, :] - y_recv[ITERS - 1, here, :].astype(jnp.float32)
        save = pltpu.make_async_copy(
            grad.at[pl.ds(face + p * piece, piece)],
            grad_hbm.at[0, pl.ds(p * piece, piece)],
            out_sem.at[1 + p],
        )
        save.start()
        saves.append(save)
    for copy in sent:
        copy.wait_send()
    for save in saves:
        save.wait()


def on_device(operators, dual_rhs, contact, costs):
    n = lax.axis_size("wide")
    order = operators.shape[2]
    face, cases = dual_rhs.shape[1:]
    f32, bf16 = jnp.float32, jnp.bfloat16
    chunks = 2 * PIECES
    shape = jax.ShapeDtypeStruct(dual_rhs.shape, f32)
    return pl.pallas_call(
        functools.partial(kernel, n),
        out_shape=(shape, shape),
        in_specs=[
            pl.BlockSpec(memory_space=pl.ANY),
            pl.BlockSpec(memory_space=pl.ANY),
            pl.BlockSpec(memory_space=pltpu.VMEM),
            pl.BlockSpec(memory_space=pltpu.SMEM),
        ],
        out_specs=(
            pl.BlockSpec(memory_space=pl.ANY),
            pl.BlockSpec(memory_space=pl.ANY),
        ),
        scratch_shapes=[
            pltpu.VMEM((order, order), bf16),
            pltpu.VMEM((face, cases), f32),
            pltpu.VMEM((face, cases), bf16),
            pltpu.VMEM((face, cases), bf16),
            pltpu.VMEM((1, face), jnp.int32),
            pltpu.VMEM((order, cases), f32),
            pltpu.VMEM((order, cases), f32),
            pltpu.VMEM((order, cases), f32),
            pltpu.VMEM((order, cases), bf16),
            pltpu.VMEM((ITERS, order, cases), bf16),
            pltpu.VMEM((ITERS, order, cases), bf16),
            pltpu.VMEM((ITERS, 2, cases), f32),
            pltpu.VMEM((ITERS, n, 2, cases), f32),
            pltpu.SemaphoreType.DMA((2,)),
            pltpu.SemaphoreType.DMA((1 + PIECES,)),
            pltpu.SemaphoreType.DMA((1 + PIECES,)),
            pltpu.SemaphoreType.DMA((1 + PIECES,)),
            pltpu.SemaphoreType.DMA((ITERS, chunks)),
            pltpu.SemaphoreType.DMA((ITERS, chunks)),
            pltpu.SemaphoreType.DMA((ITERS, n)),
            pltpu.SemaphoreType.DMA((ITERS, n)),
        ],
        compiler_params=pltpu.CompilerParams(
            collective_id=0,
            has_side_effects=True,
            vmem_limit_bytes=60 * 1024 * 1024,
        ),
        cost_estimate=pl.CostEstimate(
            flops=2 * ITERS * order * order * cases,
            bytes_accessed=2 * order * order + 12 * face * cases,
            transcendentals=0,
        ),
    )(operators, dual_rhs, contact, costs)


def solution(mesh):
    return jax.shard_map(
        on_device,
        mesh=mesh,
        in_specs=(
            P("lend", "wide", None, None),
            P("lend", "wide", None),
            P("lend", "wide"),
            P("lend", "wide"),
        ),
        out_specs=(P("lend", "wide", None), P("lend", "wide", None)),
        check_vma=False,
    )
```

time: 188 us -> 46.2 us (0.25)
  blocking collectives: 57.7 us -> 0 us
  waiting for transfers between devices: 57.5 us -> 0 us
  Pallas kernels: 0 us -> 41.4 us
  matrix products: 37.5 us -> 0 us
  loops' own time: 24.2 us -> 0 us
  other arithmetic: 4.6 us -> 0 us
  starting transfers between devices: 4.06 us -> 0 us
  local copies, waits for them, and re-layouts: 0.23 us -> 3.34 us
    psum x3 -> x0, blocking collectives: 57.7 us -> none  [on_device(): denom = lax.psum(bending, 'wide')]
    ppermute x8 -> x0, waiting for transfers between devices: 57.5 us -> none  [from_behind(): return lax.ppermute(block, axis, route)]
    pallas_call x0 -> x1, Pallas kernels: none -> 41.4 us  [on_device(): pl.pallas_call(functools.partial(kernel, n), out_shape=(shape, shape), in...]
    dot_general x32 -> x0, matrix products: 37.5 us -> none  [add_block(): piece = jnp.dot(rows_here, vectors, preferred_element_type=jnp.float32)]
    another operation x4 -> x0, loops' own time: 24.2 us -> none  [block_product(): return lax.fori_loop(start_block, stop_block, add_block, empty)]
    ppermute x8 -> x0, starting transfers between devices: 4.06 us -> none  [from_behind(): return lax.ppermute(block, axis, route)]
    unnamed x2, local copies, waits for them, and re-layouts: 0.01 us -> 3.34 us
  transfers between devices with their start and end apart: 8 -> 0, of which waited for: 8 -> 0; matrix products, arithmetic and copies ran while one was open for 0% -> 0% of each run, Pallas kernels for 0% -> 0%
where the time goes in v1:
time: 46.2 us; the launch traced here: 46 us
  Pallas kernels  41.4 us (90%)
  local copies, waits for them, and re-layouts  3.34 us (7%)
  between operations  1.29 us (3%)
    pallas_call x1, Pallas kernels, on_device(): pl.pallas_call(functools.partial(kernel, n), out_shape=(shape, shape), in...  41.4 us
    unnamed x2, local copies, waits for them, and re-layouts  3.34 us

profile of v1, /device:TPU:0, one launch (start us, length us, event | category | flops | bytes accessed | tf_op | source)
XLA Modules:
  0.0 46.0 jit_solution(14798440450766918462)
XLA Ops:
  1.3 41.4 %shard_map.59 = (f32[1,512,128]{2,1,0:T(8,128)}, f32[1,512,128]{2,1,0:T(8,128)}) custom-call(bf16[1,1,1024,1024]{3,2,1,0:T(8,128)(2,1)} %op_hbm.1, f32[1,512,128]{2,1,0:T(8,128)} %rhs_hbm.1, s32[1,512]{1,0:T(1,128)} %contact_ref.1, s32[1,1]{1,0:T(1,128)S(6)} %copy.8.costs_ref), custom_call_target="tpu_custom_call" | custom-call | flops 1073741824 | bytes 2883584 | tf_op jit(solution)/shard_map/pallas_call | solution.py:253
  42.7 1.7 %copy.9 = f32[1,512,128]{2,1,0:T(8,128)} copy(f32[1,512,128]{2,1,0:T(8,128)} %get-tuple-element.4) | data formatting | bytes 524288
  44.3 1.7 %copy.10 = f32[1,512,128]{2,1,0:T(8,128)} copy(f32[1,512,128]{2,1,0:T(8,128)} %get-tuple-element.5) | data formatting | bytes 524288

commit v2 on v1

v2 whole, which is shorter than its diff:
```python
import functools

import jax
import jax.numpy as jnp
from jax import lax
from jax.experimental import pallas as pl
from jax.experimental.pallas import tpu as pltpu
from jax.sharding import PartitionSpec as P

ROWBLK = 128
ITERS = 4
RIDGE = 1.0
FIRST_STEP = 0.1
EPSILON = 1e-06
PIECES = 2
MESH = pl.DeviceIdType.MESH


def kernel(
    n,
    op_hbm,
    rhs_hbm,
    contact_ref,
    costs_ref,
    lam_hbm,
    grad_hbm,
    op,
    rhs,
    rhs_send,
    rhs_recv,
    facts_send,
    facts_recv,
    floor,
    lam,
    grad,
    operand,
    product,
    y_send,
    top_recv,
    pair_recv,
    low_send,
    low_recv,
    part_send,
    part_recv,
    load_sem,
    out_sem,
    first_send_sem,
    first_recv_sem,
    top_send_sem,
    top_recv_sem,
    low_send_sem,
    low_recv_sem,
    part_send_sem,
    part_recv_sem,
):
    order, cases = operand.shape
    face = order // 2
    piece = face // PIECES
    me = lax.axis_index("wide")
    right = {"wide": lax.rem(me + 1, n)}
    left = {"wide": lax.rem(me + n - 1, n)}
    lend = lax.axis_index("lend")
    side = lax.rem(lend, 2)
    pair = {"lend": lend + 1 - 2 * side}
    mine = pl.ds(pl.multiple_of(side * piece, piece), piece)
    theirs = pl.ds(pl.multiple_of((1 - side) * piece, piece), piece)
    sent = []

    def send(src, dst, send_sem, recv_sem, where):
        copy = pltpu.make_async_remote_copy(
            src_ref=src,
            dst_ref=dst,
            send_sem=send_sem,
            recv_sem=recv_sem,
            device_id=where,
            device_id_type=MESH,
        )
        copy.start()
        sent.append(copy)
        return copy

    load_rhs = pltpu.make_async_copy(rhs_hbm.at[0], rhs, load_sem.at[0])
    load_rhs.start()
    load_op = pltpu.make_async_copy(op_hbm.at[0, 0], op, load_sem.at[1])
    load_op.start()

    barrier = pltpu.get_barrier_semaphore()
    for d in range(1, n):
        pl.semaphore_signal(
            barrier, inc=1, device_id={"wide": lax.rem(me + d, n)}, device_id_type=MESH
        )
    pl.semaphore_signal(barrier, inc=1, device_id=pair, device_id_type=MESH)

    live = costs_ref[0, 0] * ROWBLK

    def active(start, rows, count):
        return lax.broadcasted_iota(jnp.int32, (rows, cases), 0) + start < count

    def make_floor(flags, base):
        for start in range(0, face, ROWBLK):
            row = flags[0:1, start : start + ROWBLK]
            row = jnp.where(row == 1, 0.0, -jnp.inf).astype(jnp.float32)
            floor[base + start : base + start + ROWBLK, :] = jnp.broadcast_to(
                row, (cases, ROWBLK)
            ).T

    facts_send[0:1, :] = contact_ref[...]
    facts_send[1:2, :] = jnp.full((1, face), live, jnp.int32)
    load_rhs.wait()
    rhs_send[...] = rhs[...].astype(jnp.bfloat16)

    pl.semaphore_wait(barrier, n)

    facts = send(
        facts_send, facts_recv, first_send_sem.at[PIECES], first_recv_sem.at[PIECES], right
    )
    first = []
    for p in range(PIECES):
        rows = pl.ds(p * piece, piece)
        first.append(
            send(
                rhs_send.at[rows],
                rhs_recv.at[rows],
                first_send_sem.at[p],
                first_recv_sem.at[p],
                right,
            )
        )

    def advance(base, start, rows, steplen, gradient_at, begins):
        squares = jnp.zeros((8, cases), jnp.float32)
        for here in range(start, start + rows, ROWBLK):
            at = slice(base + here, base + here + ROWBLK)
            g = gradient_at(here)
            before = jnp.zeros_like(g) if begins else lam[at, :]
            moved = jnp.maximum(before - steplen * g, floor[at, :])
            change = moved - before
            lam[at, :] = moved
            grad[at, :] = g + RIDGE * change
            squares += jnp.sum((change * change).reshape(ROWBLK // 8, 8, cases), axis=0)
            signed = change if base else -change
            operand[at, :] = jnp.where(
                active(base + here, ROWBLK, live), signed, 0.0
            ).astype(jnp.bfloat16)
        return squares

    def multiply(start, columns, begins):
        vectors = operand[start : start + columns, :]
        for r in range(0, order, piece):
            part = jnp.dot(
                op[r : r + piece, start : start + columns],
                vectors,
                preferred_element_type=jnp.float32,
            )
            at = slice(r, r + piece)
            product[at, :] = part if begins else product[at, :] + part

    make_floor(contact_ref, face)
    steplen = jnp.full((1, cases), FIRST_STEP, jnp.float32)
    tops = lows = None
    live_left = None
    for it in range(ITERS):
        finished = it + 1 == ITERS
        if it == 0:
            squares = advance(face, 0, face, steplen, lambda i: -rhs[i : i + ROWBLK, :], True)
            load_op.wait()
            multiply(face, face, True)
            facts.wait_recv()
            make_floor(facts_recv, 0)
            live_left = facts_recv[1:2, 0:cases]
            for p in range(PIECES):
                first[p].wait_recv()
                advance(
                    0,
                    p * piece,
                    piece,
                    steplen,
                    lambda i: -rhs_recv[i : i + ROWBLK, :].astype(jnp.float32),
                    True,
                )
                if p + 1 < PIECES:
                    multiply(p * piece, piece, False)
            last = (PIECES - 1) * piece
        else:

            def own_gradient(i, it=it):
                came = top_recv[it - 1, i : i + ROWBLK, :].astype(jnp.float32)
                return grad[face + i : face + i + ROWBLK, :] - came

            def left_gradient(i, it=it):
                came = low_recv[it - 1, i : i + ROWBLK, :].astype(jnp.float32)
                came = jnp.where(active(face + i, ROWBLK, live_left), came, 0.0)
                return grad[i : i + ROWBLK, :] + came

            squares = jnp.zeros((8, cases), jnp.float32)
            for p in range(PIECES):
                if p + 1 == PIECES:
                    lows.wait_recv()
                    forward = send(
                        low_recv.at[it - 1, mine],
                        low_recv.at[it - 1, mine],
                        low_send_sem.at[it - 1, 2],
                        low_recv_sem.at[it - 1, 2],
                        pair,
                    )
                    forward.wait_recv()
                    advance(0, 0, face, steplen, left_gradient, False)
                    multiply(0, face, False)
                tops[p].wait_recv()
                squares += advance(face, p * piece, piece, steplen, own_gradient, False)
                if p + 1 < PIECES:
                    multiply(face + p * piece, piece, p == 0)
            last = face + (PIECES - 1) * piece
        if finished:
            save_lam = pltpu.make_async_copy(
                lam.at[pl.ds(face, face)], lam_hbm.at[0], out_sem.at[0]
            )
            save_lam.start()

        bending = RIDGE * squares
        tops = []
        vectors = operand[last : last + piece, :]
        for r in list(range(face, order, piece)) + list(range(0, face, piece)):
            at = slice(r, r + piece)
            y = product[at, :] + jnp.dot(
                op[at, last : last + piece], vectors, preferred_element_type=jnp.float32
            )
            y = jnp.where(active(r, piece, live), y, 0.0)
            product[at, :] = y
            if finished and r >= face:
                continue
            y_send[it, at, :] = y.astype(jnp.bfloat16)
            if not finished:
                bending += jnp.sum(
                    (operand[at, :].astype(jnp.float32) * y).reshape(
                        piece // 8, 8, cases
                    ),
                    axis=0,
                )
                if r + piece == order:
                    swap = send(
                        y_send.at[it, pl.ds(pl.multiple_of(face + (1 - side) * piece, piece), piece)],
                        pair_recv.at[it],
                        low_send_sem.at[it, 0],
                        low_recv_sem.at[it, 0],
                        pair,
                    )

        def send_top(p):
            rows = pl.ds(p * piece, piece)
            tops.append(
                send(
                    y_send.at[it, rows],
                    top_recv.at[it, rows],
                    top_send_sem.at[it, p],
                    top_recv_sem.at[it, p],
                    left,
                )
            )

        if finished:
            for p in range(PIECES):
                send_top(p)
            grad[face:, :] = grad[face:, :] + product[face:, :]
        else:
            own = jnp.concatenate(
                [
                    jnp.sum(squares, axis=0, keepdims=True),
                    jnp.sum(bending, axis=0, keepdims=True),
                ],
                axis=0,
            )
            part_send[it] = own
            parts = [
                send(
                    part_send.at[it],
                    part_recv.at[it, d],
                    part_send_sem.at[it, d],
                    part_recv_sem.at[it, d],
                    {"wide": lax.rem(me + d, n)},
                )
                for d in range(1, n)
            ]
            for p in range(PIECES - 1):
                send_top(p)
            swap.wait_recv()
            low_mine = pl.ds(pl.multiple_of(face + side * piece, piece), piece)
            low_send[it] = y_send[it, low_mine, :] + pair_recv[it]
            lows = send(
                low_send.at[it],
                low_recv.at[it, mine],
                low_send_sem.at[it, 1],
                low_recv_sem.at[it, 1],
                right,
            )
            send_top(PIECES - 1)
            grad[:face, :] = grad[:face, :] - product[:face, :]
            grad[face:, :] = grad[face:, :] + product[face:, :]
            total = own
            for d in range(1, n):
                parts[d - 1].wait_recv()
                total = total + part_recv[it, d]
            steplen = (total[0:1] + EPSILON) / (total[1:2] + EPSILON)

    saves = [save_lam]
    for p in range(PIECES):
        tops[p].wait_recv()
        at = slice(face + p * piece, face + (p + 1) * piece)
        here = slice(p * piece, (p + 1) * piece)
        grad[at, :] = grad[at, :] - top_recv[ITERS - 1, here, :].astype(jnp.float32)
        save = pltpu.make_async_copy(
            grad.at[pl.ds(face + p * piece, piece)],
            grad_hbm.at[0, pl.ds(p * piece, piece)],
            out_sem.at[1 + p],
        )
        save.start()
        saves.append(save)
    for copy in sent:
        copy.wait_send()
    for save in saves:
        save.wait()


def on_device(operators, dual_rhs, contact, costs):
    n = lax.axis_size("wide")
    order = operators.shape[2]
    face, cases = dual_rhs.shape[1:]
    f32, bf16 = jnp.float32, jnp.bfloat16
    piece = face // PIECES
    shape = jax.ShapeDtypeStruct(dual_rhs.shape, f32)
    return pl.pallas_call(
        functools.partial(kernel, n),
        out_shape=(shape, shape),
        in_specs=[
            pl.BlockSpec(memory_space=pl.ANY),
            pl.BlockSpec(memory_space=pl.ANY),
            pl.BlockSpec(memory_space=pltpu.VMEM),
            pl.BlockSpec(memory_space=pltpu.SMEM),
        ],
        out_specs=(
            pl.BlockSpec(memory_space=pl.ANY),
            pl.BlockSpec(memory_space=pl.ANY),
        ),
        scratch_shapes=[
            pltpu.VMEM((order, order), bf16),
            pltpu.VMEM((face, cases), f32),
            pltpu.VMEM((face, cases), bf16),
            pltpu.VMEM((face, cases), bf16),
            pltpu.VMEM((2, face), jnp.int32),
            pltpu.VMEM((2, face), jnp.int32),
            pltpu.VMEM((order, cases), f32),
            pltpu.VMEM((order, cases), f32),
            pltpu.VMEM((order, cases), f32),
            pltpu.VMEM((order, cases), bf16),
            pltpu.VMEM((order, cases), f32),
            pltpu.VMEM((ITERS, order, cases), bf16),
            pltpu.VMEM((ITERS, face, cases), bf16),
            pltpu.VMEM((ITERS, piece, cases), bf16),
            pltpu.VMEM((ITERS, piece, cases), bf16),
            pltpu.VMEM((ITERS, face, cases), bf16),
            pltpu.VMEM((ITERS, 2, cases), f32),
            pltpu.VMEM((ITERS, n, 2, cases), f32),
            pltpu.SemaphoreType.DMA((2,)),
            pltpu.SemaphoreType.DMA((1 + PIECES,)),
            pltpu.SemaphoreType.DMA((1 + PIECES,)),
            pltpu.SemaphoreType.DMA((1 + PIECES,)),
            pltpu.SemaphoreType.DMA((ITERS, PIECES)),
            pltpu.SemaphoreType.DMA((ITERS, PIECES)),
            pltpu.SemaphoreType.DMA((ITERS, 3)),
            pltpu.SemaphoreType.DMA((ITERS, 3)),
            pltpu.SemaphoreType.DMA((ITERS, n)),
            pltpu.SemaphoreType.DMA((ITERS, n)),
        ],
        compiler_params=pltpu.CompilerParams(
            collective_id=0,
            has_side_effects=True,
            vmem_limit_bytes=52 * 1024 * 1024,
        ),
        cost_estimate=pl.CostEstimate(
            flops=2 * ITERS * order * order * cases,
            bytes_accessed=2 * order * order + 12 * face * cases,
            transcendentals=0,
        ),
    )(operators, dual_rhs, contact, costs)


def solution(mesh):
    return jax.shard_map(
        on_device,
        mesh=mesh,
        in_specs=(
            P("lend", "wide", None, None),
            P("lend", "wide", None),
            P("lend", "wide"),
            P("lend", "wide"),
        ),
        out_specs=(P("lend", "wide", None), P("lend", "wide", None)),
        check_vma=False,
    )
```

time: 46.2 us -> 45.4 us (0.983)
  Pallas kernels: 41.4 us -> 40.9 us
    pallas_call x1, Pallas kernels: 41.4 us -> 40.9 us  [on_device(): pl.pallas_call(functools.partial(kernel, n), out_shape=(shape, shape), in...]
    unnamed x2 -> x6, local copies, waits for them, and re-layouts: 3.34 us -> 3.03 us
where the time goes in v2:
time: 45.4 us; the launch traced here: 45.2 us
  Pallas kernels  40.9 us (90%)
  local copies, waits for them, and re-layouts  3.03 us (7%)
  between operations  1.29 us (3%)
    pallas_call x1, Pallas kernels, on_device(): pl.pallas_call(functools.partial(kernel, n), out_shape=(shape, shape), in...  40.9 us
    unnamed x6, local copies, waits for them, and re-layouts  3.03 us

profile of v2, /device:TPU:0, one launch (start us, length us, event | category | flops | bytes accessed | tf_op | source)
XLA Modules:
  0.0 45.2 jit_solution(6724240048227146173)
XLA Ops:
  1.3 0.0 copy-start
  1.3 0.9 %copy-done = f32[1,512,128]{2,1,0:T(8,128)S(1)} copy-done((f32[1,512,128]{2,1,0:T(8,128)S(1)}, f32[1,512,128]{2,1,0:T(8,128)}, u32[]{:S(2)}) %copy-start) | copy-done | bytes 262168
  2.2 0.0 copy-start.1
  2.2 0.7 %copy-done.1 = s32[1,512]{1,0:T(1,128)S(1)} copy-done((s32[1,512]{1,0:T(1,128)S(1)}, s32[1,512]{1,0:T(1,128)}, u32[]{:S(2)}) %copy-start.1) | copy-done | bytes 2072
  2.9 40.9 %shard_map.59 = (f32[1,512,128]{2,1,0:T(8,128)S(1)}, f32[1,512,128]{2,1,0:T(8,128)S(1)}) custom-call(bf16[1,1,1024,1024]{3,2,1,0:T(8,128)(2,1)} %op_hbm.1, f32[1,512,128]{2,1,0:T(8,128)S(1)} %copy-done, s32[1,512]{1,0:T(1,128)S(1)} %copy-done.1, s32[1,1]{1,0:T(1,128)S(6)} %copy.8.costs_ref), custom_call_target="tpu_custom_call" | custom-call | flops 1073741824 | bytes 2883584 | tf_op jit(solution)/shard_map/pallas_call | solution.py:331
  43.8 0.7 %copy.9 = f32[1,512,128]{2,1,0:T(8,128)} copy(f32[1,512,128]{2,1,0:T(8,128)S(1)} %get-tuple-element.4) | data formatting | bytes 524288
  44.5 0.7 %copy.10 = f32[1,512,128]{2,1,0:T(8,128)} copy(f32[1,512,128]{2,1,0:T(8,128)S(1)} %get-tuple-element.5) | data formatting | bytes 524288
Async XLA Ops:
  1.3 1.0 %copy-start = (f32[1,512,128]{2,1,0:T(8,128)S(1)}, f32[1,512,128]{2,1,0:T(8,128)}, u32[]{:S(2)}) copy-start(f32[1,512,128]{2,1,0:T(8,128)} %rhs_hbm.1) | copy-start | bytes 786436
  2.2 0.7 %copy-start.1 = (s32[1,512]{1,0:T(1,128)S(1)}, s32[1,512]{1,0:T(1,128)}, u32[]{:S(2)}) copy-start(s32[1,512]{1,0:T(1,128)} %contact_ref.1) | copy-start | bytes 6148

commit v3 on v0

v3 whole, which is shorter than its diff:
```python
import functools

import jax
import jax.numpy as jnp
from jax import lax
from jax.experimental import pallas as pl
from jax.experimental.pallas import tpu as pltpu
from jax.sharding import PartitionSpec as P

ROWBLK = 128
ITERS = 4
RIDGE = 1.0
FIRST_STEP = 0.1
EPSILON = 1e-06
PARTS = 2
MESH = pl.DeviceIdType.MESH


def kernel(
    n,
    op_hbm,
    rhs_hbm,
    contact_hbm,
    costs_ref,
    lam_hbm,
    grad_hbm,
    op,
    rhs,
    own_rhs,
    rhs_send,
    rhs_recv,
    contact,
    contact_recv,
    floor,
    lam,
    grad,
    field,
    operand,
    out,
    y_send,
    top_recv,
    low_recv,
    part_send,
    part_recv,
    load_sem,
    out_sem,
    first_send_sem,
    first_recv_sem,
    y_send_sem,
    y_recv_sem,
    part_send_sem,
    part_recv_sem,
):
    order = op.shape[0]
    face, cases = rhs.shape
    rows = face // PARTS
    me = lax.axis_index("wide")
    right = {"wide": lax.rem(me + 1, n)}
    left = {"wide": lax.rem(me + n - 1, n)}
    sent = []

    def send(src, dst, send_sem, recv_sem, where):
        copy = pltpu.make_async_remote_copy(
            src_ref=src,
            dst_ref=dst,
            send_sem=send_sem,
            recv_sem=recv_sem,
            device_id=where,
            device_id_type=MESH,
        )
        copy.start()
        sent.append(copy)
        return copy

    load_rhs = pltpu.make_async_copy(rhs_hbm.at[0], rhs, load_sem.at[0])
    load_rhs.start()
    load_contact = pltpu.make_async_copy(contact_hbm, contact, load_sem.at[1])
    load_contact.start()
    load_op = pltpu.make_async_copy(op_hbm.at[0, 0], op, load_sem.at[2])
    load_op.start()

    barrier = pltpu.get_barrier_semaphore()
    for d in range(1, n):
        pl.semaphore_signal(
            barrier, inc=1, device_id={"wide": lax.rem(me + d, n)}, device_id_type=MESH
        )

    def first_lanes(count):
        return lax.broadcasted_iota(jnp.int32, (count, cases), 1) < cases // 2

    def swap(values):
        return pltpu.roll(values, cases // 2, axis=1)

    def active(start, count):
        row = lax.broadcasted_iota(jnp.int32, (count, cases), 0) + start
        return jnp.where(first_lanes(count), row, row + rows) < live

    def exchange(upper, lower, half):
        first = first_lanes(upper.shape[0])
        if half == 0:
            return jnp.where(first, upper, swap(lower))
        return jnp.where(first, swap(upper), lower)

    def make_floor(flags, base):
        for start in range(0, rows, ROWBLK):
            both = [
                jnp.broadcast_to(
                    jnp.where(flags[0:1, at : at + ROWBLK] == 1, 0.0, -jnp.inf).astype(
                        jnp.float32
                    ),
                    (cases // 2, ROWBLK),
                )
                for at in (start, start + rows)
            ]
            floor[base + start : base + start + ROWBLK, :] = jnp.concatenate(
                both, axis=0
            ).T

    load_rhs.wait()
    for half in range(2):
        packed = exchange(rhs[0:rows, :], rhs[rows:face, :], half)
        own_rhs[half] = packed
        rhs_send[half] = packed.astype(jnp.bfloat16)
    load_contact.wait()
    live = costs_ref[0, 0] * ROWBLK

    pl.semaphore_wait(barrier, n - 1)

    first = [
        send(
            rhs_send.at[half],
            rhs_recv.at[half],
            first_send_sem.at[half],
            first_recv_sem.at[half],
            right,
        )
        for half in range(2)
    ]
    facts = send(contact, contact_recv, first_send_sem.at[2], first_recv_sem.at[2], right)

    def advance(half, own, steplen, gradient_at, begins):
        base = rows if own else 0
        squares = jnp.zeros((8, cases), jnp.float32)
        for here in range(0, rows, ROWBLK):
            at = slice(base + here, base + here + ROWBLK)
            g = gradient_at(here)
            before = jnp.zeros_like(g) if begins else lam[half, at, :]
            moved = jnp.maximum(before - steplen * g, floor[at, :])
            change = moved - before
            lam[half, at, :] = moved
            grad[half, at, :] = g + RIDGE * change
            if own:
                squares += jnp.sum(
                    (change * change).reshape(ROWBLK // 8, 8, cases), axis=0
                )
            masked = jnp.where(
                active(2 * base + here, ROWBLK), change if own else -change, 0.0
            )
            field[half, at, :] = masked
            turned = swap(masked)
            lanes = first_lanes(ROWBLK)
            slot = 2 * base + here
            operand[half, slot : slot + ROWBLK, :] = jnp.where(
                lanes, masked, turned
            ).astype(jnp.bfloat16)
            operand[half, slot + rows : slot + rows + ROWBLK, :] = jnp.where(
                lanes, turned, masked
            ).astype(jnp.bfloat16)
        return squares

    def fold(sums):
        total = jnp.sum(sums, axis=0, keepdims=True)
        return total + swap(total)

    steplen = [jnp.full((1, cases), FIRST_STEP, jnp.float32)] * 2
    make_floor(contact, rows)
    squares = [
        advance(
            half,
            True,
            steplen[half],
            lambda i, half=half: -own_rhs[half, i : i + ROWBLK, :],
            True,
        )
        for half in range(2)
    ]
    facts.wait_recv()
    make_floor(contact_recv, 0)
    tops, lows, parts, sums = [None] * 2, [None] * 2, [None] * 2, [None] * 2
    for it in range(ITERS):
        finished = it + 1 == ITERS
        for half in range(2):
            if it == 0:
                first[half].wait_recv()
                advance(
                    half,
                    False,
                    steplen[half],
                    lambda i: -rhs_recv[half, i : i + ROWBLK, :].astype(jnp.float32),
                    True,
                )
            else:
                total = sums[half]
                for d in range(1, n):
                    parts[half][d - 1].wait_recv()
                    total = total + part_recv[it - 1, half, d]
                steplen[half] = (total[0:1] + EPSILON) / (total[1:2] + EPSILON)

                def own_gradient(i):
                    came = top_recv[it - 1, half, i : i + ROWBLK, :]
                    at = slice(rows + i, rows + i + ROWBLK)
                    return grad[half, at, :] - came.astype(jnp.float32)

                def left_gradient(i):
                    came = low_recv[it - 1, half, i : i + ROWBLK, :]
                    at = slice(i, i + ROWBLK)
                    return grad[half, at, :] + came.astype(jnp.float32)

                tops[half].wait_recv()
                squares[half] = advance(half, True, steplen[half], own_gradient, False)
                lows[half].wait_recv()
                advance(half, False, steplen[half], left_gradient, False)
            if it == 0 and half == 0:
                load_op.wait()

            bending = RIDGE * squares[half]
            for base in (0, rows):
                y = jnp.dot(
                    op[2 * base : 2 * base + face, :],
                    operand[half],
                    preferred_element_type=jnp.float32,
                )
                y = jnp.where(first_lanes(rows), y[0:rows, :], y[rows:face, :])
                y = jnp.where(active(2 * base, rows), y, 0.0)
                at = slice(base, base + rows)
                if not finished or base == 0:
                    y_send[it, half, at, :] = y.astype(jnp.bfloat16)
                if base == 0:
                    tops[half] = send(
                        y_send.at[it, half, pl.ds(0, rows)],
                        top_recv.at[it, half],
                        y_send_sem.at[it, half, 0],
                        y_recv_sem.at[it, half, 0],
                        left,
                    )
                    if not finished:
                        grad[half, at, :] = grad[half, at, :] - y
                else:
                    grad[half, at, :] = grad[half, at, :] + y
                if not finished:
                    bending += jnp.sum(
                        (field[half, at, :] * y).reshape(rows // 8, 8, cases), axis=0
                    )
            if finished:
                continue
            sums[half] = jnp.concatenate([fold(squares[half]), fold(bending)], axis=0)
            part_send[it, half] = sums[half]
            parts[half] = [
                send(
                    part_send.at[it, half],
                    part_recv.at[it, half, d],
                    part_send_sem.at[it, half, d],
                    part_recv_sem.at[it, half, d],
                    {"wide": lax.rem(me + d, n)},
                )
                for d in range(1, n)
            ]
            lows[half] = send(
                y_send.at[it, half, pl.ds(rows, rows)],
                low_recv.at[it, half],
                y_send_sem.at[it, half, 1],
                y_recv_sem.at[it, half, 1],
                right,
            )

    def unpack(source):
        return [
            exchange(source[0, rows:face, :], source[1, rows:face, :], part)
            for part in range(2)
        ]

    saves = []

    def save(number, values, target):
        for part in range(2):
            out[number, part * rows : (part + 1) * rows, :] = values[part]
        copy = pltpu.make_async_copy(out.at[number], target.at[0], out_sem.at[number])
        copy.start()
        saves.append(copy)

    save(0, unpack(lam), lam_hbm)
    for half in range(2):
        tops[half].wait_recv()
        came = top_recv[ITERS - 1, half].astype(jnp.float32)
        grad[half, rows:face, :] = grad[half, rows:face, :] - came
    save(1, unpack(grad), grad_hbm)
    for copy in sent:
        copy.wait_send()
    for copy in saves:
        copy.wait()


def write_out(lam, grad, lam_out, grad_out, sem):
    copies = [
        pltpu.make_async_copy(lam, lam_out, sem.at[0]),
        pltpu.make_async_copy(grad, grad_out, sem.at[1]),
    ]
    for copy in copies:
        copy.start()
    for copy in copies:
        copy.wait()


def on_device(operators, dual_rhs, contact, costs):
    n = lax.axis_size("wide")
    order = operators.shape[2]
    face, cases = dual_rhs.shape[1:]
    rows = face // PARTS
    f32, bf16 = jnp.float32, jnp.bfloat16
    shape = jax.ShapeDtypeStruct(dual_rhs.shape, f32)
    inputs = [
        pltpu.with_memory_space_constraint(x, pltpu.HBM)
        for x in (operators, dual_rhs, contact)
    ]
    results = pl.pallas_call(
        functools.partial(kernel, n),
        out_shape=(shape, shape),
        in_specs=[
            pl.BlockSpec(memory_space=pl.ANY),
            pl.BlockSpec(memory_space=pl.ANY),
            pl.BlockSpec(memory_space=pl.ANY),
            pl.BlockSpec(memory_space=pltpu.SMEM),
        ],
        out_specs=(
            pl.BlockSpec(memory_space=pl.ANY),
            pl.BlockSpec(memory_space=pl.ANY),
        ),
        scratch_shapes=[
            pltpu.VMEM((order, order), bf16),
            pltpu.VMEM((face, cases), f32),
            pltpu.VMEM((2, rows, cases), f32),
            pltpu.VMEM((2, rows, cases), bf16),
            pltpu.VMEM((2, rows, cases), bf16),
            pltpu.VMEM((1, face), jnp.int32),
            pltpu.VMEM((1, face), jnp.int32),
            pltpu.VMEM((face, cases), f32),
            pltpu.VMEM((2, face, cases), f32),
            pltpu.VMEM((2, face, cases), f32),
            pltpu.VMEM((2, face, cases), f32),
            pltpu.VMEM((2, order, cases), bf16),
            pltpu.VMEM((2, face, cases), f32),
            pltpu.VMEM((ITERS, 2, face, cases), bf16),
            pltpu.VMEM((ITERS, 2, rows, cases), bf16),
            pltpu.VMEM((ITERS, 2, rows, cases), bf16),
            pltpu.VMEM((ITERS, 2, 2, cases), f32),
            pltpu.VMEM((ITERS, 2, n, 2, cases), f32),
            pltpu.SemaphoreType.DMA((3,)),
            pltpu.SemaphoreType.DMA((2,)),
            pltpu.SemaphoreType.DMA((3,)),
            pltpu.SemaphoreType.DMA((3,)),
            pltpu.SemaphoreType.DMA((ITERS, 2, 2)),
            pltpu.SemaphoreType.DMA((ITERS, 2, 2)),
            pltpu.SemaphoreType.DMA((ITERS, 2, n)),
            pltpu.SemaphoreType.DMA((ITERS, 2, n)),
        ],
        compiler_params=pltpu.CompilerParams(
            collective_id=0,
            has_side_effects=True,
            vmem_limit_bytes=52 * 1024 * 1024,
        ),
        cost_estimate=pl.CostEstimate(
            flops=2 * ITERS * order * order * cases,
            bytes_accessed=2 * order * order + 12 * face * cases,
            transcendentals=0,
        ),
    )(*inputs, costs)
    return pl.pallas_call(
        write_out,
        out_shape=(shape, shape),
        in_specs=[pl.BlockSpec(memory_space=pl.ANY)] * 2,
        out_specs=(pl.BlockSpec(memory_space=pl.ANY),) * 2,
        scratch_shapes=[pltpu.SemaphoreType.DMA((2,))],
    )(*results)


def solution(mesh):
    return jax.shard_map(
        on_device,
        mesh=mesh,
        in_specs=(
            P("lend", "wide", None, None),
            P("lend", "wide", None),
            P("lend", "wide"),
            P("lend", "wide"),
        ),
        out_specs=(P("lend", "wide", None), P("lend", "wide", None)),
        check_vma=False,
    )
```

time: 188 us -> 58.7 us (0.31)
  blocking collectives: 57.7 us -> 0 us
  waiting for transfers between devices: 57.5 us -> 0 us
  Pallas kernels: 0 us -> 55.8 us
  matrix products: 37.5 us -> 0 us
  loops' own time: 24.2 us -> 0 us
  other arithmetic: 4.6 us -> 0 us
  starting transfers between devices: 4.06 us -> 0 us
    psum x3 -> x0, blocking collectives: 57.7 us -> none  [on_device(): denom = lax.psum(bending, 'wide')]
    ppermute x8 -> x0, waiting for transfers between devices: 57.5 us -> none  [from_behind(): return lax.ppermute(block, axis, route)]
    pallas_call x0 -> x2, Pallas kernels: none -> 55.8 us  [the longest x1 38.8 us: on_device(): pl.pallas_call(functools.partial(kernel, n), out_shape=(shape, shape), in...]
    dot_general x32 -> x0, matrix products: 37.5 us -> none  [add_block(): piece = jnp.dot(rows_here, vectors, preferred_element_type=jnp.float32)]
    another operation x4 -> x0, loops' own time: 24.2 us -> none  [block_product(): return lax.fori_loop(start_block, stop_block, add_block, empty)]
    ppermute x8 -> x0, starting transfers between devices: 4.06 us -> none  [from_behind(): return lax.ppermute(block, axis, route)]
  transfers between devices with their start and end apart: 8 -> 0, of which waited for: 8 -> 0; matrix products, arithmetic and copies ran while one was open for 0% -> 0% of each run, Pallas kernels for 0% -> 0%
where the time goes in v3:
time: 58.7 us; the launch traced here: 58.5 us
  Pallas kernels  55.8 us (95%)
  local copies, waits for them, and re-layouts  1.39 us (2%)
  between operations  1.29 us (2%)
    pallas_call x1, Pallas kernels, on_device(): pl.pallas_call(functools.partial(kernel, n), out_shape=(shape, shape), in...  38.8 us
    pallas_call x1, Pallas kernels, on_device(): pl.pallas_call(write_out, out_shape=(shape, shape), in_specs=[pl.BlockSpe...  17 us
    unnamed x4, local copies, waits for them, and re-layouts  1.39 us

profile of v3, /device:TPU:0, one launch (start us, length us, event | category | flops | bytes accessed | tf_op | source)
XLA Modules:
  0.0 58.5 jit_solution(17888736433144201249)
XLA Ops:
  1.3 38.8 %shard_map.59 = (f32[1,512,128]{2,1,0:T(8,128)S(1)}, f32[1,512,128]{2,1,0:T(8,128)S(1)}) custom-call(bf16[1,1,1024,1024]{3,2,1,0:T(8,128)(2,1)} %op_hbm.1, f32[1,512,128]{2,1,0:T(8,128)} %rhs_hbm.1, s32[1,512]{1,0:T(1,128)} %contact_hbm.1, s32[1,1]{1,0:T(1,128)S(6)} %copy.6.costs_ref), custom_call_target="tpu_custom_call" | custom-call | flops 1073741824 | bytes 2883584 | tf_op jit(solution)/shard_map/pallas_call | solution.py:325
  40.1 0.0 copy-start
  40.1 0.7 %copy-done = f32[1,512,128]{2,1,0:T(8,128)} copy-done((f32[1,512,128]{2,1,0:T(8,128)}, f32[1,512,128]{2,1,0:T(8,128)S(1)}, u32[]{:S(2)}) %copy-start) | copy-done | bytes 262168
  40.8 0.0 copy-start.1
  40.8 0.7 %copy-done.1 = f32[1,512,128]{2,1,0:T(8,128)} copy-done((f32[1,512,128]{2,1,0:T(8,128)}, f32[1,512,128]{2,1,0:T(8,128)S(1)}, u32[]{:S(2)}) %copy-start.1) | copy-done | bytes 262168
  41.5 17.0 %shard_map.60 = (f32[1,512,128]{2,1,0:T(8,128)}, f32[1,512,128]{2,1,0:T(8,128)}) custom-call(f32[1,512,128]{2,1,0:T(8,128)} %copy-done, f32[1,512,128]{2,1,0:T(8,128)} %copy-done.1), custom_call_target="tpu_custom_call" | custom-call | tf_op jit(solution)/shard_map/pallas_call | solution.py:377
Async XLA Ops:
  40.1 0.7 %copy-start = (f32[1,512,128]{2,1,0:T(8,128)}, f32[1,512,128]{2,1,0:T(8,128)S(1)}, u32[]{:S(2)}) copy-start(f32[1,512,128]{2,1,0:T(8,128)S(1)} %get-tuple-element.4.lam) | copy-start | bytes 786436
  40.8 0.7 %copy-start.1 = (f32[1,512,128]{2,1,0:T(8,128)}, f32[1,512,128]{2,1,0:T(8,128)S(1)}, u32[]{:S(2)}) copy-start(f32[1,512,128]{2,1,0:T(8,128)S(1)} %get-tuple-element.5.grad) | copy-start | bytes 786436

commit v4 on v3

--- a/solution.py
+++ b/solution.py
@@ -30,7 +30,8 @@
     rhs_send,
     rhs_recv,
     contact,
-    contact_recv,
+    facts_send,
+    facts_recv,
     floor,
     lam,
     grad,
@@ -39,6 +40,8 @@
     out,
     y_send,
     top_recv,
+    pair_recv,
+    low_send,
     low_recv,
     part_send,
     part_recv,
@@ -48,6 +51,8 @@
     first_recv_sem,
     y_send_sem,
     y_recv_sem,
+    low_send_sem,
+    low_recv_sem,
     part_send_sem,
     part_recv_sem,
 ):
@@ -57,6 +62,12 @@
     me = lax.axis_index("wide")
     right = {"wide": lax.rem(me + 1, n)}
     left = {"wide": lax.rem(me + n - 1, n)}
+    lend = lax.axis_index("lend")
+    side = lax.rem(lend, 2)
+    pair = {"lend": lend + 1 - 2 * side}
+    share = rows // 2
+    mine = pl.multiple_of(side * share, share)
+    theirs = pl.multiple_of((1 - side) * share, share)
     sent = []
 
     def send(src, dst, send_sem, recv_sem, where):
@@ -85,15 +96,17 @@
             barrier, inc=1, device_id={"wide": lax.rem(me + d, n)}, device_id_type=MESH
         )
 
+    pl.semaphore_signal(barrier, inc=1, device_id=pair, device_id_type=MESH)
+
     def first_lanes(count):
         return lax.broadcasted_iota(jnp.int32, (count, cases), 1) < cases // 2
 
     def swap(values):
         return pltpu.roll(values, cases // 2, axis=1)
 
-    def active(start, count):
+    def active(start, count, bound):
         row = lax.broadcasted_iota(jnp.int32, (count, cases), 0) + start
-        return jnp.where(first_lanes(count), row, row + rows) < live
+        return jnp.where(first_lanes(count), row, row + rows) < bound
 
     def exchange(upper, lower, half):
         first = first_lanes(upper.shape[0])
@@ -123,8 +136,10 @@
         rhs_send[half] = packed.astype(jnp.bfloat16)
     load_contact.wait()
     live = costs_ref[0, 0] * ROWBLK
-
-    pl.semaphore_wait(barrier, n - 1)
+    facts_send[0:1, :] = contact[...]
+    facts_send[1:2, :] = jnp.full((1, face), live, jnp.int32)
+
+    pl.semaphore_wait(barrier, n)
 
     first = [
         send(
@@ -136,7 +151,7 @@
         )
         for half in range(2)
     ]
-    facts = send(contact, contact_recv, first_send_sem.at[2], first_recv_sem.at[2], right)
+    facts = send(facts_send, facts_recv, first_send_sem.at[2], first_recv_sem.at[2], right)
 
     def advance(half, own, steplen, gradient_at, begins):
         base = rows if own else 0
@@ -154,7 +169,7 @@
                     (change * change).reshape(ROWBLK // 8, 8, cases), axis=0
                 )
             masked = jnp.where(
-                active(2 * base + here, ROWBLK), change if own else -change, 0.0
+                active(2 * base + here, ROWBLK, live), change if own else -change, 0.0
             )
             field[half, at, :] = masked
             turned = swap(masked)
@@ -185,8 +200,10 @@
         for half in range(2)
     ]
     facts.wait_recv()
-    make_floor(contact_recv, 0)
-    tops, lows, parts, sums = [None] * 2, [None] * 2, [None] * 2, [None] * 2
+    make_floor(facts_recv, 0)
+    live_left = facts_recv[1:2, 0:cases]
+    tops, swaps, lows = [None] * 2, [None] * 2, [None] * 2
+    parts, sums = [None] * 2, [None] * 2
     for it in range(ITERS):
         finished = it + 1 == ITERS
         for half in range(2):
@@ -200,6 +217,14 @@
                     True,
                 )
             else:
+                lows[half].wait_recv()
+                forward = send(
+                    low_recv.at[it - 1, half, pl.ds(mine, share)],
+                    low_recv.at[it - 1, half, pl.ds(mine, share)],
+                    low_send_sem.at[it - 1, half, 2],
+                    low_recv_sem.at[it - 1, half, 2],
+                    pair,
+                )
                 total = sums[half]
                 for d in range(1, n):
                     parts[half][d - 1].wait_recv()
@@ -212,26 +237,27 @@
                     return grad[half, at, :] - came.astype(jnp.float32)
 
                 def left_gradient(i):
-                    came = low_recv[it - 1, half, i : i + ROWBLK, :]
+                    came = low_recv[it - 1, half, i : i + ROWBLK, :].astype(jnp.float32)
+                    ours = active(face + i, ROWBLK, live_left)
                     at = slice(i, i + ROWBLK)
-                    return grad[half, at, :] + came.astype(jnp.float32)
+                    return grad[half, at, :] + jnp.where(ours, came, 0.0)
 
                 tops[half].wait_recv()
                 squares[half] = advance(half, True, steplen[half], own_gradient, False)
-                lows[half].wait_recv()
+                forward.wait_recv()
                 advance(half, False, steplen[half], left_gradient, False)
             if it == 0 and half == 0:
                 load_op.wait()
 
             bending = RIDGE * squares[half]
-            for base in (0, rows):
+            for base in (0, rows) if finished else (rows, 0):
                 y = jnp.dot(
                     op[2 * base : 2 * base + face, :],
                     operand[half],
                     preferred_element_type=jnp.float32,
                 )
                 y = jnp.where(first_lanes(rows), y[0:rows, :], y[rows:face, :])
-                y = jnp.where(active(2 * base, rows), y, 0.0)
+                y = jnp.where(active(2 * base, rows, live), y, 0.0)
                 at = slice(base, base + rows)
                 if not finished or base == 0:
                     y_send[it, half, at, :] = y.astype(jnp.bfloat16)
@@ -239,13 +265,21 @@
                     tops[half] = send(
                         y_send.at[it, half, pl.ds(0, rows)],
                         top_recv.at[it, half],
-                        y_send_sem.at[it, half, 0],
-                        y_recv_sem.at[it, half, 0],
+                        y_send_sem.at[it, half],
+                        y_recv_sem.at[it, half],
                         left,
                     )
                     if not finished:
                         grad[half, at, :] = grad[half, at, :] - y
                 else:
+                    if not finished:
+                        swaps[half] = send(
+                            y_send.at[it, half, pl.ds(rows + theirs, share)],
+                            pair_recv.at[it, half],
+                            low_send_sem.at[it, half, 0],
+                            low_recv_sem.at[it, half, 0],
+                            pair,
+                        )
                     grad[half, at, :] = grad[half, at, :] + y
                 if not finished:
                     bending += jnp.sum(
@@ -265,11 +299,15 @@
                 )
                 for d in range(1, n)
             ]
+            swaps[half].wait_recv()
+            low_send[it, half] = (
+                y_send[it, half, pl.ds(rows + mine, share), :] + pair_recv[it, half]
+            )
             lows[half] = send(
-                y_send.at[it, half, pl.ds(rows, rows)],
-                low_recv.at[it, half],
-                y_send_sem.at[it, half, 1],
-                y_recv_sem.at[it, half, 1],
+                low_send.at[it, half],
+                low_recv.at[it, half, pl.ds(mine, share)],
+                low_send_sem.at[it, half, 1],
+                low_recv_sem.at[it, half, 1],
                 right,
             )
 
@@ -297,17 +335,6 @@
     for copy in sent:
         copy.wait_send()
     for copy in saves:
-        copy.wait()
-
-
-def write_out(lam, grad, lam_out, grad_out, sem):
-    copies = [
-        pltpu.make_async_copy(lam, lam_out, sem.at[0]),
-        pltpu.make_async_copy(grad, grad_out, sem.at[1]),
-    ]
-    for copy in copies:
-        copy.start()
-    for copy in copies:
         copy.wait()
 
 
@@ -322,7 +349,7 @@
         pltpu.with_memory_space_constraint(x, pltpu.HBM)
         for x in (operators, dual_rhs, contact)
     ]
-    results = pl.pallas_call(
+    return pl.pallas_call(
         functools.partial(kernel, n),
         out_shape=(shape, shape),
         in_specs=[
@@ -342,7 +369,8 @@
             pltpu.VMEM((2, rows, cases), bf16),
             pltpu.VMEM((2, rows, cases), bf16),
             pltpu.VMEM((1, face), jnp.int32),
-            pltpu.VMEM((1, face), jnp.int32),
+            pltpu.VMEM((2, face), jnp.int32),
+            pltpu.VMEM((2, face), jnp.int32),
             pltpu.VMEM((face, cases), f32),
             pltpu.VMEM((2, face, cases), f32),
             pltpu.VMEM((2, face, cases), f32),
@@ -351,6 +379,8 @@
             pltpu.VMEM((2, face, cases), f32),
             pltpu.VMEM((ITERS, 2, face, cases), bf16),
             pltpu.VMEM((ITERS, 2, rows, cases), bf16),
+            pltpu.VMEM((ITERS, 2, rows // 2, cases), bf16),
+            pltpu.VMEM((ITERS, 2, rows // 2, cases), bf16),
             pltpu.VMEM((ITERS, 2, rows, cases), bf16),
             pltpu.VMEM((ITERS, 2, 2, cases), f32),
             pltpu.VMEM((ITERS, 2, n, 2, cases), f32),
@@ -358,8 +388,10 @@
             pltpu.SemaphoreType.DMA((2,)),
             pltpu.SemaphoreType.DMA((3,)),
             pltpu.SemaphoreType.DMA((3,)),
-            pltpu.SemaphoreType.DMA((ITERS, 2, 2)),
-            pltpu.SemaphoreType.DMA((ITERS, 2, 2)),
+            pltpu.SemaphoreType.DMA((ITERS, 2)),
+            pltpu.SemaphoreType.DMA((ITERS, 2)),
+            pltpu.SemaphoreType.DMA((ITERS, 2, 3)),
+            pltpu.SemaphoreType.DMA((ITERS, 2, 3)),
             pltpu.SemaphoreType.DMA((ITERS, 2, n)),
             pltpu.SemaphoreType.DMA((ITERS, 2, n)),
         ],
@@ -374,13 +406,6 @@
             transcendentals=0,
         ),
     )(*inputs, costs)
-    return pl.pallas_call(
-        write_out,
-        out_shape=(shape, shape),
-        in_specs=[pl.BlockSpec(memory_space=pl.ANY)] * 2,
-        out_specs=(pl.BlockSpec(memory_space=pl.ANY),) * 2,
-        scratch_shapes=[pltpu.SemaphoreType.DMA((2,))],
-    )(*results)
 
 
 def solution(mesh):

time: 58.7 us -> 42.4 us (0.72)
  Pallas kernels: 55.8 us -> 39.5 us
    pallas_call x1 -> x0, Pallas kernels: 17 us -> none  [on_device(): pl.pallas_call(write_out, out_shape=(shape, shape), in_specs=[pl.BlockSpe...]
    pallas_call x1, Pallas kernels: 38.8 us -> 39.5 us  [on_device(): pl.pallas_call(functools.partial(kernel, n), out_shape=(shape, shape), in...]
    unnamed x4 -> x2, local copies, waits for them, and re-layouts: 1.39 us -> 1.41 us
where the time goes in v4:
time: 42.4 us; the launch traced here: 42.2 us
  Pallas kernels  39.5 us (93%)
  local copies, waits for them, and re-layouts  1.41 us (3%)
  between operations  1.29 us (3%)
    pallas_call x1, Pallas kernels, on_device(): pl.pallas_call(functools.partial(kernel, n), out_shape=(shape, shape), in...  39.5 us
    unnamed x2, local copies, waits for them, and re-layouts  1.41 us

profile of v4, /device:TPU:0, one launch (start us, length us, event | category | flops | bytes accessed | tf_op | source)
XLA Modules:
  0.0 42.2 jit_solution(11787014828126945640)
XLA Ops:
  1.3 39.5 %shard_map.59 = (f32[1,512,128]{2,1,0:T(8,128)S(1)}, f32[1,512,128]{2,1,0:T(8,128)S(1)}) custom-call(bf16[1,1,1024,1024]{3,2,1,0:T(8,128)(2,1)} %op_hbm.1, f32[1,512,128]{2,1,0:T(8,128)} %rhs_hbm.1, s32[1,512]{1,0:T(1,128)} %contact_hbm.1, s32[1,1]{1,0:T(1,128)S(6)} %copy.8.costs_ref), custom_call_target="tpu_custom_call" | custom-call | flops 1073741824 | bytes 2883584 | tf_op jit(solution)/shard_map/pallas_call | solution.py:352
  40.8 0.7 %copy.9 = f32[1,512,128]{2,1,0:T(8,128)} copy(f32[1,512,128]{2,1,0:T(8,128)S(1)} %get-tuple-element.4) | data formatting | bytes 524288
  41.5 0.7 %copy.10 = f32[1,512,128]{2,1,0:T(8,128)} copy(f32[1,512,128]{2,1,0:T(8,128)S(1)} %get-tuple-element.5) | data formatting | bytes 524288

commit v5 on v3

--- a/solution.py
+++ b/solution.py
@@ -59,7 +59,7 @@
     left = {"wide": lax.rem(me + n - 1, n)}
     sent = []
 
-    def send(src, dst, send_sem, recv_sem, where):
+    def send(src, dst, send_sem, recv_sem, where, at_once=True):
         copy = pltpu.make_async_remote_copy(
             src_ref=src,
             dst_ref=dst,
@@ -68,7 +68,8 @@
             device_id=where,
             device_id_type=MESH,
         )
-        copy.start()
+        if at_once:
+            copy.start()
         sent.append(copy)
         return copy
 
@@ -201,8 +202,9 @@
                 )
             else:
                 total = sums[half]
+                for copy in parts[half]:
+                    copy.wait_recv()
                 for d in range(1, n):
-                    parts[half][d - 1].wait_recv()
                     total = total + part_recv[it - 1, half, d]
                 steplen[half] = (total[0:1] + EPSILON) / (total[1:2] + EPSILON)
 
@@ -242,6 +244,7 @@
                         y_send_sem.at[it, half, 0],
                         y_recv_sem.at[it, half, 0],
                         left,
+                        finished,
                     )
                     if not finished:
                         grad[half, at, :] = grad[half, at, :] - y
@@ -255,16 +258,18 @@
                 continue
             sums[half] = jnp.concatenate([fold(squares[half]), fold(bending)], axis=0)
             part_send[it, half] = sums[half]
-            parts[half] = [
-                send(
-                    part_send.at[it, half],
-                    part_recv.at[it, half, d],
-                    part_send_sem.at[it, half, d],
-                    part_recv_sem.at[it, half, d],
-                    {"wide": lax.rem(me + d, n)},
-                )
-                for d in range(1, n)
-            ]
+            parts[half] = []
+            for d in range(1, n):
+                parts[half].append(
+                    send(
+                        part_send.at[it, half],
+                        part_recv.at[it, half, d],
+                        part_send_sem.at[it, half, d],
+                        part_recv_sem.at[it, half, d],
+                        {"wide": lax.rem(me + d, n)},
+                    )
+                )
+            tops[half].start()
             lows[half] = send(
                 y_send.at[it, half, pl.ds(rows, rows)],
                 low_recv.at[it, half],
@@ -297,17 +302,6 @@
     for copy in sent:
         copy.wait_send()
     for copy in saves:
-        copy.wait()
-
-
-def write_out(lam, grad, lam_out, grad_out, sem):
-    copies = [
-        pltpu.make_async_copy(lam, lam_out, sem.at[0]),
-        pltpu.make_async_copy(grad, grad_out, sem.at[1]),
-    ]
-    for copy in copies:
-        copy.start()
-    for copy in copies:
         copy.wait()
 
 
@@ -322,7 +316,7 @@
         pltpu.with_memory_space_constraint(x, pltpu.HBM)
         for x in (operators, dual_rhs, contact)
     ]
-    results = pl.pallas_call(
+    return pl.pallas_call(
         functools.partial(kernel, n),
         out_shape=(shape, shape),
         in_specs=[
@@ -374,13 +368,6 @@
             transcendentals=0,
         ),
     )(*inputs, costs)
-    return pl.pallas_call(
-        write_out,
-        out_shape=(shape, shape),
-        in_specs=[pl.BlockSpec(memory_space=pl.ANY)] * 2,
-        out_specs=(pl.BlockSpec(memory_space=pl.ANY),) * 2,
-        scratch_shapes=[pltpu.SemaphoreType.DMA((2,))],
-    )(*results)
 
 
 def solution(mesh):

time: 58.7 us -> 42.5 us (0.72)
  Pallas kernels: 55.8 us -> 39.6 us
    pallas_call x1 -> x0, Pallas kernels: 17 us -> none  [on_device(): pl.pallas_call(write_out, out_shape=(shape, shape), in_specs=[pl.BlockSpe...]
    pallas_call x1, Pallas kernels: 38.8 us -> 39.6 us  [on_device(): pl.pallas_call(functools.partial(kernel, n), out_shape=(shape, shape), in...]
    unnamed x4 -> x2, local copies, waits for them, and re-layouts: 1.39 us -> 1.41 us
where the time goes in v5:
time: 42.5 us; the launch traced here: 42.3 us
  Pallas kernels  39.6 us (93%)
  local copies, waits for them, and re-layouts  1.41 us (3%)
  between operations  1.29 us (3%)
    pallas_call x1, Pallas kernels, on_device(): pl.pallas_call(functools.partial(kernel, n), out_shape=(shape, shape), in...  39.6 us
    unnamed x2, local copies, waits for them, and re-layouts  1.41 us

profile of v5, /device:TPU:0, one launch (start us, length us, event | category | flops | bytes accessed | tf_op | source)
XLA Modules:
  0.0 42.3 jit_solution(6951639152521031881)
XLA Ops:
  1.3 39.6 %shard_map.59 = (f32[1,512,128]{2,1,0:T(8,128)S(1)}, f32[1,512,128]{2,1,0:T(8,128)S(1)}) custom-call(bf16[1,1,1024,1024]{3,2,1,0:T(8,128)(2,1)} %op_hbm.1, f32[1,512,128]{2,1,0:T(8,128)} %rhs_hbm.1, s32[1,512]{1,0:T(1,128)} %contact_hbm.1, s32[1,1]{1,0:T(1,128)S(6)} %copy.8.costs_ref), custom_call_target="tpu_custom_call" | custom-call | flops 1073741824 | bytes 2883584 | tf_op jit(solution)/shard_map/pallas_call | solution.py:319
  40.9 0.7 %copy.9 = f32[1,512,128]{2,1,0:T(8,128)} copy(f32[1,512,128]{2,1,0:T(8,128)S(1)} %get-tuple-element.4) | data formatting | bytes 524288
  41.6 0.7 %copy.10 = f32[1,512,128]{2,1,0:T(8,128)} copy(f32[1,512,128]{2,1,0:T(8,128)S(1)} %get-tuple-element.5) | data formatting | bytes 524288

commit v6 on v4

--- a/solution.py
+++ b/solution.py
@@ -70,7 +70,7 @@
     theirs = pl.multiple_of((1 - side) * share, share)
     sent = []
 
-    def send(src, dst, send_sem, recv_sem, where):
+    def send(src, dst, send_sem, recv_sem, where, at_once=True):
         copy = pltpu.make_async_remote_copy(
             src_ref=src,
             dst_ref=dst,
@@ -79,7 +79,8 @@
             device_id=where,
             device_id_type=MESH,
         )
-        copy.start()
+        if at_once:
+            copy.start()
         sent.append(copy)
         return copy
 
@@ -226,8 +227,9 @@
                     pair,
                 )
                 total = sums[half]
+                for copy in parts[half]:
+                    copy.wait_recv()
                 for d in range(1, n):
-                    parts[half][d - 1].wait_recv()
                     total = total + part_recv[it - 1, half, d]
                 steplen[half] = (total[0:1] + EPSILON) / (total[1:2] + EPSILON)
 
@@ -268,6 +270,7 @@
                         y_send_sem.at[it, half],
                         y_recv_sem.at[it, half],
                         left,
+                        finished,
                     )
                     if not finished:
                         grad[half, at, :] = grad[half, at, :] - y
@@ -289,16 +292,18 @@
                 continue
             sums[half] = jnp.concatenate([fold(squares[half]), fold(bending)], axis=0)
             part_send[it, half] = sums[half]
-            parts[half] = [
-                send(
-                    part_send.at[it, half],
-                    part_recv.at[it, half, d],
-                    part_send_sem.at[it, half, d],
-                    part_recv_sem.at[it, half, d],
-                    {"wide": lax.rem(me + d, n)},
-                )
-                for d in range(1, n)
-            ]
+            parts[half] = []
+            for d in sorted(range(1, n), key=lambda d: -min(d, n - d)):
+                parts[half].append(
+                    send(
+                        part_send.at[it, half],
+                        part_recv.at[it, half, d],
+                        part_send_sem.at[it, half, d],
+                        part_recv_sem.at[it, half, d],
+                        {"wide": lax.rem(me + d, n)},
+                    )
+                )
+            tops[half].start()
             swaps[half].wait_recv()
             low_send[it, half] = (
                 y_send[it, half, pl.ds(rows + mine, share), :] + pair_recv[it, half]

time: 42.4 us -> 42.5 us (level)
  no operation moved by 1% of the time
where the time goes in v6:
time: 42.5 us; the launch traced here: 42.4 us
  Pallas kernels  39.7 us (93%)
  local copies, waits for them, and re-layouts  1.41 us (3%)
  between operations  1.29 us (3%)
    pallas_call x1, Pallas kernels, on_device(): pl.pallas_call(functools.partial(kernel, n), out_shape=(shape, shape), in...  39.7 us
    unnamed x2, local copies, waits for them, and re-layouts  1.41 us

profile of v6, /device:TPU:0, one launch (start us, length us, event | category | flops | bytes accessed | tf_op | source)
XLA Modules:
  0.0 42.4 jit_solution(15979716705592900325)
XLA Ops:
  1.3 39.7 %shard_map.59 = (f32[1,512,128]{2,1,0:T(8,128)S(1)}, f32[1,512,128]{2,1,0:T(8,128)S(1)}) custom-call(bf16[1,1,1024,1024]{3,2,1,0:T(8,128)(2,1)} %op_hbm.1, f32[1,512,128]{2,1,0:T(8,128)} %rhs_hbm.1, s32[1,512]{1,0:T(1,128)} %contact_hbm.1, s32[1,1]{1,0:T(1,128)S(6)} %copy.8.costs_ref), custom_call_target="tpu_custom_call" | custom-call | flops 1073741824 | bytes 2883584 | tf_op jit(solution)/shard_map/pallas_call | solution.py:357
  40.9 0.7 %copy.9 = f32[1,512,128]{2,1,0:T(8,128)} copy(f32[1,512,128]{2,1,0:T(8,128)S(1)} %get-tuple-element.4) | data formatting | bytes 524288
  41.7 0.7 %copy.10 = f32[1,512,128]{2,1,0:T(8,128)} copy(f32[1,512,128]{2,1,0:T(8,128)S(1)} %get-tuple-element.5) | data formatting | bytes 524288
